TPU v7x, 256 devices: a whole 4x4x8 slice. The times are simulated.
256 devices in a mesh: region: 8 (over x, core), sub: 32 (over z, y).
Axes of the slice: x: 4, y: 4, z: 8, core: 2. Of those that a mesh axis runs over, the one named last changes fastest.
Arguments:
- features: bfloat16 [1048576, 128], P(('region', 'sub')), may hold values from -6 to 6
- face_rows: int32 [512, 256], P(('region', 'sub')), may hold values from 0 to 4095
- sub_send: int32 [8192, 64], P(('region', 'sub')), may hold values from 0 to 4608, as said below
- neighbors: int32 [1048576, 27], P(('region', 'sub')), may hold values from 0 to 6656, as said below
- w_sub: bfloat16 [3456, 128], replicated, may hold values from -0.15625 to 0.15625
- parent_position: int32 [1048576], P(('region', 'sub')), may hold values from 0 to 7
- coarse_target: int32 [1048576], P(('region', 'sub')), may hold values from 0 to 16383, as said below
- w_down: bfloat16 [1024, 128], replicated, may hold values from -0.5 to 0.5
Outputs:
- fine: bfloat16 [1048576, 128], P(('region', 'sub'))
- coarse: bfloat16 [131072, 128], P(('region', 'sub'))
Inputs may be any that keep to these rules, and one draw needn't show every extreme that they name: `sub_send`: toward each index of sub a device lists its live rows first and 4608 after them; nothing toward itself; toward the next index of sub, wrapping, all 64 slots are live. `neighbors`: rows of received blocks are only live slots; offset 27 // 2 is the voxel itself. `coarse_target`: at most 157 rows of one device have targets owned by any one other index of sub (target // 512); every device reaches it.
All inputs are finite; a program needn't handle non-finite values.
Results may differ from a plain program's by a relative error of at most 0.0065.
Values may be sent and summed in bfloat16 or wider, within the bound.
A program may use at most 64 MiB of HBM per device.

v0:
```python
import jax
import jax.numpy as jnp
from jax import lax
from jax.sharding import PartitionSpec as P


def from_behind(block, axis, distance):
    devices = range(lax.axis_size(axis))
    route = [(i - distance, i) for i in devices if i - distance in devices]
    return lax.ppermute(block, axis, route)


def convolve(full_table, kernel_maps, features, w_sub):
    voxel_count, width = features.shape
    block_rows = min(512, voxel_count)
    block_count = voxel_count // block_rows

    def one_block(argument_list):
        map_block, input_block = argument_list
        gathered = full_table[map_block].reshape(block_rows, -1)
        summed = jnp.dot(gathered, w_sub, preferred_element_type=jnp.float32)
        return jax.nn.relu(input_block.astype(jnp.float32) + summed).astype(jnp.bfloat16)

    blocks = lax.map(
        one_block,
        (
            kernel_maps.reshape(block_count, block_rows, -1),
            features.reshape(block_count, block_rows, width),
        ),
    )
    return blocks.reshape(voxel_count, width)


def project_down(rows, offsets, w_down):
    row_count, width = rows.shape
    chosen = offsets[:, None, None] == jnp.arange(8, dtype=jnp.int32)[None, :, None]
    expanded = jnp.where(chosen, rows[:, None, :], jnp.zeros((), jnp.bfloat16)).reshape(
        row_count, 8 * width
    )
    return jnp.dot(expanded, w_down, preferred_element_type=jnp.float32)


def accumulate(target_ids, rows, dest_count):
    onehot = (jnp.arange(dest_count, dtype=jnp.int32)[:, None] == target_ids[None, :]).astype(
        jnp.float32
    )
    return jnp.dot(
        onehot, rows, precision=lax.Precision.HIGHEST, preferred_element_type=jnp.float32
    )


def plan_slots(owner, sub_count, capacity, self_index):
    voxel_count = owner.shape[0]
    block_rows = min(512, voxel_count)
    block_count = voxel_count // block_rows
    slot_count = sub_count * capacity
    lower = (jnp.arange(block_rows)[:, None] > jnp.arange(block_rows)[None, :]).astype(jnp.bfloat16)
    targets = jnp.arange(sub_count, dtype=jnp.int32)
    slot_ids = jnp.arange(slot_count, dtype=jnp.int32)

    def step(carry, argument_list):
        counts, source = carry
        owner_block, start = argument_list
        matches = owner_block[:, None] == targets[None, :]
        before = (
            jnp.dot(lower, matches.astype(jnp.bfloat16), preferred_element_type=jnp.float32)
            + counts[None, :]
        )
        ranking = jnp.sum(jnp.where(matches, before, 0.0), 1).astype(jnp.int32)
        remote_block = owner_block != self_index
        slot_block = jnp.where(remote_block, owner_block * capacity + ranking, slot_count)
        row_ids = start + jnp.arange(block_rows, dtype=jnp.int32)
        hit = slot_ids[:, None] == slot_block[None, :]
        source = jnp.maximum(source, jnp.max(jnp.where(hit, row_ids[None, :], -1), 1))
        counts = counts + jnp.sum(matches.astype(jnp.float32), 0)
        return ((counts, source), None)

    starts = jnp.arange(block_count, dtype=jnp.int32) * block_rows
    initial = (jnp.zeros((sub_count,), jnp.float32), jnp.full((slot_count,), -1, jnp.int32))
    (counts, source), unused = lax.scan(
        step, initial, (owner.reshape(block_count, block_rows), starts)
    )
    filled = source >= 0
    return (owner != self_index, jnp.maximum(source, 0), filled)


def per_device(
    features, face_rows, sub_send, neighbors, w_sub, parent_position, coarse_target, w_down
):
    voxel_count, width = features.shape
    sent_low = features[face_rows[0]]
    sent_high = features[face_rows[1]]
    from_below = from_behind(sent_high, "region", 1)
    from_above = from_behind(sent_low, "region", -1)
    blank_row = jnp.zeros((1, width), jnp.bfloat16)
    table = jnp.concatenate([features, from_below, from_above, blank_row], 0)
    sub_count = lax.axis_size("sub")
    outgoing = table[sub_send.reshape(-1)].reshape(sub_count, -1, width)
    incoming = lax.all_to_all(outgoing, "sub", split_axis=0, concat_axis=0, tiled=True)
    full_table = jnp.concatenate([table, incoming.reshape(-1, width)], 0)
    fine = convolve(full_table, neighbors, features, w_sub)
    coarse_count = voxel_count // 8
    owner = coarse_target // coarse_count
    within = coarse_target - owner * coarse_count
    capacity = voxel_count // 32 + (voxel_count // 4 - voxel_count // 32 + sub_count - 2) // (
        sub_count - 1
    )
    self_index = lax.axis_index("sub")
    remote, source, filled = plan_slots(owner, sub_count, capacity, self_index)
    local_ids = jnp.where(remote, coarse_count, within)
    partial_result = project_down(fine, parent_position, w_down)
    packed = jnp.where(filled[:, None], partial_result[source], 0.0).reshape(
        sub_count, capacity, width
    )
    packed_ids = jnp.where(filled, within[source], coarse_count).reshape(sub_count, capacity)
    onehot = (
        jnp.arange(coarse_count, dtype=jnp.int32)[None, :, None] == packed_ids[:, None, :]
    ).astype(jnp.float32)
    remote_sums = jnp.einsum(
        "sjc,scd->sjd",
        onehot,
        packed,
        precision=lax.Precision.HIGHEST,
        preferred_element_type=jnp.float32,
    )
    local_sums = accumulate(local_ids, partial_result, coarse_count)
    own_block = (jnp.arange(sub_count, dtype=jnp.int32) == self_index)[:, None, None]
    spread = (remote_sums + jnp.where(own_block, local_sums[None], 0.0)).reshape(
        sub_count * coarse_count, width
    )
    summed = lax.psum_scatter(spread, "sub", scatter_dimension=0, tiled=True)
    return (fine, summed.astype(jnp.bfloat16))


def solution(mesh):
    return jax.shard_map(
        per_device,
        mesh=mesh,
        in_specs=(
            P(("region", "sub"), None),
            P(("region", "sub"), None),
            P(("region", "sub"), None),
            P(("region", "sub"), None),
            P(),
            P(("region", "sub")),
            P(("region", "sub")),
            P(),
        ),
        out_specs=(P(("region", "sub"), None), P(("region", "sub"), None)),
        check_vma=False,
    )
```

profile of v0, /device:TPU:2, one launch (start us, length us, event | category | flops | bytes accessed | tf_op | source)
XLA Modules:
  0.0 739.0 jit_solution(3726623188297578013)
XLA Ops:
  8.0 2.1 gather_fusion.1
  10.1 1.9 collective-permute-start
  12.0 2.1 gather_fusion.2
  14.1 3.6 collective-permute-start.1
  19.9 26.0 %while.24 = (s32[]{:T(128)}, f32[32]{0:T(128)S(1)}, s32[5024]{0:T(1024)S(1)}, s32[8,512]{1,0:T(8,128)S(1)}, s32[]{:T(128)}, /*index=5*/s32[8]{0:T(128)S(1)}, s32[]{:T(128)}, s32[]{:T(128)}) while((s32[]{:T(128)}, f32[32]{0:T(128)S(1)}, s32[5024]{0:T(1024)S(1)}, s32[8,512]{1,0:T(8,128)S(1)}, s32[]{:T(128)}, ...), condition=%wide.region_6.7_spmd.clone, body=%wide.region_2.6_spmd.clone.sunk | while | flops 25157060 | bytes 107900 | solution.py:80
  21.6 1.5 select_reduce_fusion.2
  24.9 1.5 select_reduce_fusion.2
  31.4 1.5 select_reduce_fusion.2
  37.9 1.5 select_reduce_fusion.2
  44.4 1.5 select_reduce_fusion.2
  46.1 8.0 %gather_fusion.3 = bf16[2048,128]{1,0:T(8,128)(2,1)} fusion(bf16[4609,128]{1,0:T(8,128)(2,1)S(1)} %pad_maximum_fusion, s32[2048]{0:T(1024)S(1)} %broadcast_clamp_fusion), kind=kCustom, calls=%fused_computation.3 | custom fusion | bytes 1056768 | tf_op jit(solution)/shard_map/gather | solution.py:98
  54.1 11.5 %all-to-all-start = ((bf16[32,64,128]{2,1,0:T(8,128)(2,1)}), bf16[32,64,128]{2,1,0:T(8,128)(2,1)S(1)}, u32[]{:S(2)}, u32[]{:S(2)}) async-start(bf16[32,64,128]{2,1,0:T(8,128)(2,1)} %bitcast.67), calls=%async_computation | async-start | bytes 1048576 | tf_op jit(solution)/shard_map/all_to_all | solution.py:99
  65.9 3.0 copy.11
  70.4 28.4 %gather_fusion.4 = s32[5024]{0:T(1024)S(1)} fusion(s32[4096]{0:T(1024)S(1)} %get-tuple-element.140, s32[5120]{0:T(1024)S(1)} %pad_clamp_fusion.1), kind=kCustom, calls=%fused_computation.4 | custom fusion | bytes 60288 | tf_op jit(solution)/shard_map/gather | solution.py:115
  100.3 3.5 concatenate.8
  103.8 330.2 %while.23 = (s32[]{:T(128)}, bf16[8,512,128]{2,1,0:T(8,128)(2,1)}, bf16[8,512,128]{2,1,0:T(8,128)(2,1)S(1)}, s32[8,512,27]{2,1,0:T(8,128)}, bf16[6657,128]{1,0:T...) while((s32[]{:T(128)}, bf16[8,512,128]{2,1,0:T(8,128)(2,1)}, bf16[8,512,128]{2,1,0:T(8,128)(2,1)S(1)}, ...), condition=%wide.region_1.2_spmd, body=%wide.region_0.1_spmd.sunk | while | flops 453302784 | bytes 19231312 | solution.py:24
  105.1 28.5 %gather_fusion = bf16[13824,128]{1,0:T(8,128)(2,1)} fusion(bf16[6657,128]{1,0:T(8,128)(2,1)S(1)} %get-tuple-element.239, s32[14336]{0:T(1024)S(1)} %pad_clamp_fusion.5), kind=kCustom, calls=%fused_computation.clone.1 | custom fusion | bytes 7133184 | tf_op jit(solution)/shard_map/while/body/eval_jaxpr/gather | solution.py:20
  133.6 7.6 %reshape.276 = bf16[512,3456]{1,0:T(8,128)(2,1)} reshape(bf16[13824,128]{1,0:T(8,128)(2,1)} %gather_fusion) | data formatting | bytes 7077888 | tf_op jit(solution)/shard_map/while/body/eval_jaxpr/reshape | solution.py:20
  141.1 4.0 fusion.45
  146.3 28.5 %gather_fusion = bf16[13824,128]{1,0:T(8,128)(2,1)} fusion(bf16[6657,128]{1,0:T(8,128)(2,1)S(1)} %get-tuple-element.239, s32[14336]{0:T(1024)S(1)} %pad_clamp_fusion.5), kind=kCustom, calls=%fused_computation.clone.1 | custom fusion | bytes 7133184 | tf_op jit(solution)/shard_map/while/body/eval_jaxpr/gather | solution.py:20
  174.9 7.6 %reshape.276 = bf16[512,3456]{1,0:T(8,128)(2,1)} reshape(bf16[13824,128]{1,0:T(8,128)(2,1)} %gather_fusion) | data formatting | bytes 7077888 | tf_op jit(solution)/shard_map/while/body/eval_jaxpr/reshape | solution.py:20
  182.4 4.0 fusion.45
  187.6 28.5 %gather_fusion = bf16[13824,128]{1,0:T(8,128)(2,1)} fusion(bf16[6657,128]{1,0:T(8,128)(2,1)S(1)} %get-tuple-element.239, s32[14336]{0:T(1024)S(1)} %pad_clamp_fusion.5), kind=kCustom, calls=%fused_computation.clone.1 | custom fusion | bytes 7133184 | tf_op jit(solution)/shard_map/while/body/eval_jaxpr/gather | solution.py:20
  216.1 7.6 %reshape.276 = bf16[512,3456]{1,0:T(8,128)(2,1)} reshape(bf16[13824,128]{1,0:T(8,128)(2,1)} %gather_fusion) | data formatting | bytes 7077888 | tf_op jit(solution)/shard_map/while/body/eval_jaxpr/reshape | solution.py:20
  223.7 4.0 fusion.45
  228.9 28.5 %gather_fusion = bf16[13824,128]{1,0:T(8,128)(2,1)} fusion(bf16[6657,128]{1,0:T(8,128)(2,1)S(1)} %get-tuple-element.239, s32[14336]{0:T(1024)S(1)} %pad_clamp_fusion.5), kind=kCustom, calls=%fused_computation.clone.1 | custom fusion | bytes 7133184 | tf_op jit(solution)/shard_map/while/body/eval_jaxpr/gather | solution.py:20
  257.4 7.6 %reshape.276 = bf16[512,3456]{1,0:T(8,128)(2,1)} reshape(bf16[13824,128]{1,0:T(8,128)(2,1)} %gather_fusion) | data formatting | bytes 7077888 | tf_op jit(solution)/shard_map/while/body/eval_jaxpr/reshape | solution.py:20
  265.0 4.0 fusion.45
  270.2 28.5 %gather_fusion = bf16[13824,128]{1,0:T(8,128)(2,1)} fusion(bf16[6657,128]{1,0:T(8,128)(2,1)S(1)} %get-tuple-element.239, s32[14336]{0:T(1024)S(1)} %pad_clamp_fusion.5), kind=kCustom, calls=%fused_computation.clone.1 | custom fusion | bytes 7133184 | tf_op jit(solution)/shard_map/while/body/eval_jaxpr/gather | solution.py:20
  298.7 7.6 %reshape.276 = bf16[512,3456]{1,0:T(8,128)(2,1)} reshape(bf16[13824,128]{1,0:T(8,128)(2,1)} %gather_fusion) | data formatting | bytes 7077888 | tf_op jit(solution)/shard_map/while/body/eval_jaxpr/reshape | solution.py:20
  306.2 4.0 fusion.45
  311.4 28.5 %gather_fusion = bf16[13824,128]{1,0:T(8,128)(2,1)} fusion(bf16[6657,128]{1,0:T(8,128)(2,1)S(1)} %get-tuple-element.239, s32[14336]{0:T(1024)S(1)} %pad_clamp_fusion.5), kind=kCustom, calls=%fused_computation.clone.1 | custom fusion | bytes 7133184 | tf_op jit(solution)/shard_map/while/body/eval_jaxpr/gather | solution.py:20
  340.0 7.6 %reshape.276 = bf16[512,3456]{1,0:T(8,128)(2,1)} reshape(bf16[13824,128]{1,0:T(8,128)(2,1)} %gather_fusion) | data formatting | bytes 7077888 | tf_op jit(solution)/shard_map/while/body/eval_jaxpr/reshape | solution.py:20
  347.5 4.0 fusion.45
  352.7 28.5 %gather_fusion = bf16[13824,128]{1,0:T(8,128)(2,1)} fusion(bf16[6657,128]{1,0:T(8,128)(2,1)S(1)} %get-tuple-element.239, s32[14336]{0:T(1024)S(1)} %pad_clamp_fusion.5), kind=kCustom, calls=%fused_computation.clone.1 | custom fusion | bytes 7133184 | tf_op jit(solution)/shard_map/while/body/eval_jaxpr/gather | solution.py:20
  381.2 7.6 %reshape.276 = bf16[512,3456]{1,0:T(8,128)(2,1)} reshape(bf16[13824,128]{1,0:T(8,128)(2,1)} %gather_fusion) | data formatting | bytes 7077888 | tf_op jit(solution)/shard_map/while/body/eval_jaxpr/reshape | solution.py:20
  388.8 4.0 fusion.45
  394.0 28.5 %gather_fusion = bf16[13824,128]{1,0:T(8,128)(2,1)} fusion(bf16[6657,128]{1,0:T(8,128)(2,1)S(1)} %get-tuple-element.239, s32[14336]{0:T(1024)S(1)} %pad_clamp_fusion.5), kind=kCustom, calls=%fused_computation.clone.1 | custom fusion | bytes 7133184 | tf_op jit(solution)/shard_map/while/body/eval_jaxpr/gather | solution.py:20
  422.5 7.6 %reshape.276 = bf16[512,3456]{1,0:T(8,128)(2,1)} reshape(bf16[13824,128]{1,0:T(8,128)(2,1)} %gather_fusion) | data formatting | bytes 7077888 | tf_op jit(solution)/shard_map/while/body/eval_jaxpr/reshape | solution.py:20
  430.1 4.0 fusion.45
  434.0 19.9 %broadcast_select_fusion.1 = bf16[4096,8,128]{2,1,0:T(8,128)(2,1)S(1)} fusion(pred[4096,8]{1,0:T(8,128)(4,1)} %copy.12, bf16[4096,128]{1,0:T(8,128)(2,1)} %bitcast.68), kind=kLoop, calls=%fused_computation.41 | loop fusion | flops 4194304 | bytes 9469952 | tf_op jit(solution)/shard_map/jit(_where)/select_n | solution.py:37
  454.0 2.3 fusion.19
  456.4 17.7 %gather_fusion.5 = f32[5024,128]{1,0:T(8,128)} fusion(f32[4096,128]{1,0:T(8,128)S(1)} %fusion.19, s32[5120]{0:T(1024)S(1)} %copy-done.6), kind=kCustom, calls=%fused_computation.5 | custom fusion | bytes 5164672 | tf_op jit(solution)/shard_map/gather | solution.py:112
  474.1 2.9 gather.25
  477.1 4.1 fusion.22
  481.2 18.9 %select_add_fusion = f32[32,512,128]{2,1,0:T(8,128)} fusion(f32[512,128]{1,0:T(8,128)S(1)} %fusion.22, pred[32]{0:T(512)(128)(4,1)S(1)} %copy-done.10, s32[32,157]{1,0:T(8,128)S(1)} %copy-done.7, f32[32,157,128]{2,1,0:T(8,128)S(1)} %copy-done.2, pred[32,157]{1,0:T(8,128)(4,1)S(1)} %broadcast_in_dim.126), kind=kOutput, calls=%fused_computation.38 | convolution fusion | flops 3958444032 | bytes 11248192 | tf_op jit(solution)/shard_map/sjc,scd->sjd/dot_general | solution.py:119
  500.0 230.5 %reduce-scatter.2.cloned.1.call-done = f32[512,128]{1,0:T(8,128)} async-done(((f32[16384,128]{1,0:T(8,128)}), f32[512,128]{1,0:T(8,128)}) %reduce-scatter.2.cloned.1.call-update) | async-done | bytes 262160 | tf_op jit(solution)/shard_map/reduce_scatter | solution.py:131
  730.5 1.6 convert_element_type.35
  (148 shorter events, 33.9 us)
Async XLA Ops:
  7.2 446.8 %copy-start = (bf16[1024,128]{1,0:T(8,128)(2,1)S(1)}, bf16[1024,128]{1,0:T(8,128)(2,1)}, u32[]{:S(2)}) copy-start(bf16[1024,128]{1,0:T(8,128)(2,1)} %param.19) | copy-start | bytes 786436
  7.2 38.8 %copy-start.1 = (bf16[4096,128]{1,0:T(8,128)(2,1)S(1)}, bf16[4096,128]{1,0:T(8,128)(2,1)}, u32[]{:S(2)}) copy-start(bf16[4096,128]{1,0:T(8,128)(2,1)} %param.12) | copy-start | bytes 3145732
  10.1 35.8 %collective-permute-start = (bf16[256,128]{1,0:T(8,128)(2,1)S(1)}, bf16[256,128]{1,0:T(8,128)(2,1)S(1)}, u32[]{:S(2)}, u32[]{:S(2)}) collective-permute-start(bf16[256,128]{1,0:T(8,128)(2,1)S(1)} %gather_fusion.1), channel_id=1, source_target_pairs={{0,32},{32,64},{64,96},{96,128},{128,160},{160,192},{192,224},{1,3... | collective-permute-start | bytes 196616 | tf_op jit(solution)/shard_map/ppermute | solution.py:10
  14.1 31.8 %collective-permute-start.1 = (bf16[256,128]{1,0:T(8,128)(2,1)S(1)}, bf16[256,128]{1,0:T(8,128)(2,1)S(1)}, u32[]{:S(2)}, u32[]{:S(2)}) collective-permute-start(bf16[256,128]{1,0:T(8,128)(2,1)S(1)} %gather_fusion.2), channel_id=1, source_target_pairs={{32,0},{64,32},{96,64},{128,96},{160,128},{192,160},{224,192},{33,... | collective-permute-start | bytes 196616 | tf_op jit(solution)/shard_map/ppermute | solution.py:10
  45.9 8.2 %copy-start.3 = (bf16[256,128]{1,0:T(8,128)(2,1)}, bf16[256,128]{1,0:T(8,128)(2,1)S(1)}, u32[]{:S(2)}) copy-start(bf16[256,128]{1,0:T(8,128)(2,1)S(1)} %collective-permute-done) | copy-start | bytes 196612
  46.0 8.2 %copy-start.4 = (bf16[256,128]{1,0:T(8,128)(2,1)}, bf16[256,128]{1,0:T(8,128)(2,1)S(1)}, u32[]{:S(2)}) copy-start(bf16[256,128]{1,0:T(8,128)(2,1)S(1)} %collective-permute-done.1) | copy-start | bytes 196612
  46.1 19.8 %copy-start.8 = (s32[4096]{0:T(1024)S(1)}, s32[4096]{0:T(1024)}, u32[]{:S(2)}) copy-start(s32[4096]{0:T(1024)} %param.17) | copy-start | bytes 49156
  54.1 46.1 %all-to-all-start = ((bf16[32,64,128]{2,1,0:T(8,128)(2,1)}), bf16[32,64,128]{2,1,0:T(8,128)(2,1)S(1)}, u32[]{:S(2)}, u32[]{:S(2)}) async-start(bf16[32,64,128]{2,1,0:T(8,128)(2,1)} %bitcast.67), calls=%async_computation | async-start | bytes 1048576 | tf_op jit(solution)/shard_map/all_to_all | solution.py:99
  65.6 664.9 %reduce-scatter.2.cloned.1.call-start = ((), (), s32[]{:S(2)}) async-start(), calls=%async_computation.2 | async-start | bytes 8650752 | tf_op jit(solution)/shard_map/reduce_scatter | solution.py:131
  70.4 28.4 %copy-start.5 = (s32[5120]{0:T(1024)}, s32[5120]{0:T(1024)S(1)}, u32[]{:S(2)}) copy-start(s32[5120]{0:T(1024)S(1)} %pad_clamp_fusion.1) | copy-start | bytes 61444
  454.0 2.4 copy-start.6
  474.1 2.9 copy-start.9
  477.0 4.1 copy-start.2
  477.0 4.1 copy-start.7
  477.0 4.1 copy-start.10
Sparse Core Ops, SparseCore 0:
  500.2 230.3 reduce-scatter.1
where the time goes:
time: 741 us; the launch traced here: 739 us
  local copies, waits for them, and re-layouts  366 us (49%)
  waiting for transfers between devices  231 us (31%)
  matrix products  59.3 us (8%)
  other arithmetic  50.9 us (7%)
  starting transfers between devices  17.3 us (2%)
  between operations  14.3 us (2%)
    reduce_scatter x1, waiting for transfers between devices, per_device(): summed = lax.psum_scatter(spread, 'sub', scatter_dimension=0, tiled=True)  230 us
    gather x8, local copies, waits for them, and re-layouts, one_block(): gathered = full_table[map_block].reshape(block_rows, -1)  228 us
    reshape x8, local copies, waits for them, and re-layouts, one_block(): gathered = full_table[map_block].reshape(block_rows, -1)  60.4 us
    dot_general x8, matrix products, one_block(): summed = jnp.dot(gathered, w_sub, preferred_element_type=jnp.float32)  31.8 us
    gather x1, local copies, waits for them, and re-layouts, per_device(): within[source]  28.4 us
    gather x2, local copies, waits for them, and re-layouts, per_device(): partial_result[source]  20.7 us
    select_n x1, other arithmetic, project_down(): jnp.where(chosen, rows[:, None, :], jnp.zeros((), jnp.bfloat16))  19.9 us
    dot_general x1, matrix products, per_device(): jnp.einsum('sjc,scd->sjd', onehot, packed, precision=lax.Precision.HIGHES...  18.9 us
  transfers between devices with their start and end apart: 4, of which 1 were waited for; matrix products, arithmetic and copies ran while one was open for 9% of the time, Pallas kernels for 0%

commit v1 on v0

v1 whole, which is shorter than its diff:
```python
import functools

import jax
import jax.numpy as jnp
from jax import lax
from jax.experimental import pallas as pl
from jax.experimental.pallas import tpu as pltpu
from jax.sharding import PartitionSpec as P

F32, BF16, I32 = jnp.float32, jnp.bfloat16, jnp.int32
MESH = pl.DeviceIdType.MESH

WIDTH = 128
VOX = 4096
KVOL = 27
HALO = 256
PAD = VOX + 2 * HALO
RECV = PAD + 8
SUBS = 32
REGIONS = 8
CAP = 64
ROWS = RECV + SUBS * CAP
CV = VOX // 8
LANES = 128
BLOCK = 128
GROUP = 16
PARTS = ((0, 32), (32, 64), (64, 96), (96, 112), (112, 128), (128, 160))
AFTER = (9, 17, 25, 29, 32)
DEAD = VOX
NT = (((1,), (1,)), ((), ()))


def iota(shape, axis):
    return lax.broadcasted_iota(I32, shape, axis)


def exclusive_counts(onehot, upper):
    pieces, carry = [], jnp.zeros((onehot.shape[0], 1), F32)
    for start in range(0, VOX, 256):
        piece = onehot[:, start : start + 256]
        pieces.append(jnp.dot(piece, upper, preferred_element_type=F32) + carry)
        carry = carry + jnp.sum(piece.astype(F32), 1, keepdims=True)
    return jnp.concatenate(pieces, 1), carry


def plan_kernel(
    me_ref, target_ref, parent_ref, base_ref, local_ref, parent_out, place_ref,
    near_ref, far_ref, ids_ref,
):
    me = me_ref[0]
    target = target_ref[...]
    owner, within = target >> 9, target & (CV - 1)
    upper = (iota((256, 256), 0) < iota((256, 256), 1)).astype(F32).astype(BF16)
    owned = jnp.where(iota((SUBS, VOX), 0) == owner, 1.0, 0.0)
    before, _ = exclusive_counts(owned.astype(BF16), upper)
    rank = jnp.sum(owned * before, 0, keepdims=True).astype(I32)
    remote = owner != me
    part = sum((rank >= first).astype(I32) for first, _ in PARTS) - 1
    part = jnp.where(remote, part, len(PARTS))
    parts = jnp.where(iota((8, VOX), 0) == part, 1.0, 0.0)
    before, totals = exclusive_counts(parts.astype(BF16), upper)
    place = jnp.sum(
        parts * before + jnp.where(iota((8, VOX), 0) < part, totals, 0.0), 0, keepdims=True
    ).astype(I32)
    place_ref[...] = place

    def scatter(rows, values, lanes):
        stacked = jnp.concatenate([rows * v.astype(F32) for v in values], 0).astype(BF16)
        return lax.dot_general(stacked, lanes, NT, preferred_element_type=F32).astype(I32)

    voxel = iota((1, VOX), 1)
    near_id = jnp.where(remote, 0, within + 1)
    lanes = jnp.where(iota((LANES, VOX), 0) == (place & 127), 1.0, 0.0).astype(BF16)
    rows = jnp.where(iota((SUBS, VOX), 0) == (place >> 7), 1.0, 0.0)
    found = scatter(
        rows, [voxel >> 6, voxel & 63, near_id >> 5, near_id & 31, parent_ref[...]], lanes
    )
    order = found[0:32] * 64 + found[32:64]
    base_ref[...] = (order >> 7) * 1024 + (order & 127)
    local_ref[...] = found[64:96] * 32 + found[96:128]
    parent_out[...] = found[128:160].astype(F32)

    sent = jnp.where(remote, owned, 0.0)
    there = within + 1
    values = [place >> 6, place & 63, there >> 5, there & 31, jnp.ones((1, VOX), I32)]
    shifted = jnp.where(rank >= LANES, rank - LANES + 32 * (me % 4), -1)
    for which, (lane, out) in enumerate(((rank, near_ref), (shifted, far_ref))):
        lanes = jnp.where(iota((LANES, VOX), 0) == lane, 1.0, 0.0).astype(BF16)
        found = scatter(sent, values, lanes)
        out[...] = jnp.where(found[128:160] > 0, found[0:32] * 64 + found[32:64], DEAD)
        ids_ref[:, which, :] = found[64:96] * 32 + found[96:128]


def plan(me, coarse_target, parent_position):
    square = jax.ShapeDtypeStruct((SUBS, LANES), I32)
    vmem = pl.BlockSpec(memory_space=pltpu.VMEM)
    return pl.pallas_call(
        plan_kernel,
        out_shape=(
            square, square, jax.ShapeDtypeStruct((SUBS, LANES), F32),
            jax.ShapeDtypeStruct((1, VOX), I32), square, square,
            jax.ShapeDtypeStruct((SUBS, 2, LANES), I32),
        ),
        in_specs=[pl.BlockSpec(memory_space=pltpu.SMEM), vmem, vmem],
        out_specs=(vmem,) * 7,
        compiler_params=pltpu.CompilerParams(vmem_limit_bytes=48 << 20),
        name="plan",
    )(me.reshape(1), coarse_target.reshape(1, VOX), parent_position.reshape(1, VOX))


def pull(count, read, table, stage):
    for r in range(count):
        stage[r : r + 1, :] = table[pl.ds(read(r), 1), :]


def main_kernel(
    feat_hbm, face_hbm, send_hbm, maps_hbm, base_hbm, place_hbm, near_hbm, far_hbm,
    local, parent, ids, w_sub, w_down,
    fine_out, coarse_out,
    feat, face, send, maps, base, place, near, far,
    table, stage, held, sums, fine_rows, down_rows,
    halo_out, halo_in, list_out, list_in, ids_in, near_out, near_in, far_out, far_in, total,
    load_sem, halo_send, halo_recv, list_send, list_recv, ids_send, ids_recv, part_send, part_recv,
):
    region, me = lax.axis_index("region"), lax.axis_index("sub")
    below, above = lax.rem(region + REGIONS - 1, REGIONS), lax.rem(region + 1, REGIONS)
    loads = [
        pltpu.make_async_copy(source, landing, load_sem.at[i])
        for i, (source, landing) in enumerate(
            (
                (feat_hbm, feat), (face_hbm, face), (send_hbm, send), (maps_hbm, maps),
                (base_hbm, base), (place_hbm, place), (near_hbm, near), (far_hbm, far),
            )
        )
    ]
    for load in loads:
        load.start()

    barrier = pltpu.get_barrier_semaphore()
    pl.semaphore_signal(barrier, inc=1, device_id=(below, me), device_id_type=MESH)
    pl.semaphore_signal(barrier, inc=1, device_id=(above, me), device_id_type=MESH)

    def greet(d, c):
        peer = lax.rem(me + d, SUBS)
        pl.semaphore_signal(barrier, inc=1, device_id=(region, peer), device_id_type=MESH)
        return c

    lax.fori_loop(1, SUBS, greet, 0)
    table[PAD : PAD + 8, :] = jnp.zeros((8, WIDTH), F32)
    loads[0].wait()

    def widen(t, c):
        rows = pl.ds(pl.multiple_of(t * 64, 64), 64)
        table[rows, :] = feat[rows, :].astype(F32)
        return c

    lax.fori_loop(0, VOX // 64, widen, 0)
    loads[1].wait()

    def pull_face(t, c):
        pull(64, lambda r: face[t // 4, (t % 4) * 64 + r], table, stage)
        halo_out[pl.ds(pl.multiple_of(t * 64, 64), 64), :] = stage[...].astype(BF16)
        return c

    lax.fori_loop(0, 2 * HALO // 64, pull_face, 0)
    pl.semaphore_wait(barrier, SUBS + 1)

    halos = []
    for which, target in ((0, below), (1, above)):
        copy = pltpu.make_async_remote_copy(
            src_ref=halo_out.at[pl.ds(which * HALO, HALO)],
            dst_ref=halo_in.at[pl.ds((1 - which) * HALO, HALO)],
            send_sem=halo_send.at[which],
            recv_sem=halo_recv.at[which],
            device_id=(target, me),
            device_id_type=MESH,
        )
        copy.start()
        halos.append(copy)

    loads[2].wait()
    for copy in halos:
        copy.wait()
    exists_below = jnp.where(region > 0, 1.0, 0.0)
    exists_above = jnp.where(region < REGIONS - 1, 1.0, 0.0)
    table[VOX : VOX + HALO, :] = halo_in[0:HALO, :].astype(F32) * exists_below
    table[VOX + HALO : PAD, :] = halo_in[HALO:, :].astype(F32) * exists_above

    def send_list(d, c):
        peer = lax.rem(me + d, SUBS)
        pull(CAP, lambda r: send[peer, r], table, stage)
        list_out[peer] = stage[...].astype(BF16)
        pltpu.make_async_remote_copy(
            src_ref=list_out.at[peer], dst_ref=list_in.at[me],
            send_sem=list_send, recv_sem=list_recv,
            device_id=(region, peer), device_id_type=MESH,
        ).start()
        return c

    lax.fori_loop(1, SUBS, send_list, 0)

    near_in[me] = jnp.zeros((LANES, WIDTH), BF16)
    far_in[me] = jnp.zeros((32, WIDTH), BF16)
    total[...] = jnp.zeros((CV, WIDTH), F32)
    down_rows[VOX : VOX + 8, :] = jnp.zeros((8, WIDTH), F32)
    sums[...] = jnp.zeros((BLOCK, WIDTH), F32)
    for load in loads[3:]:
        load.wait()

    def settle(ref, sem):
        pltpu.make_async_copy(ref, ref, sem).wait()

    others = pl.ds(0, SUBS - 1)
    settle(list_in.at[others], list_recv)
    list_in[me] = jnp.zeros((CAP, WIDTH), BF16)

    def place_list(s, c):
        table[pl.ds(pl.multiple_of(RECV + s * CAP, 8), CAP), :] = list_in[s].astype(F32)
        return c

    lax.fori_loop(0, SUBS, place_list, 0)

    def send_ids(d, c):
        peer = lax.rem(me + d, SUBS)
        pltpu.make_async_remote_copy(
            src_ref=ids.at[peer], dst_ref=ids_in.at[me],
            send_sem=ids_send, recv_sem=ids_recv,
            device_id=(region, peer), device_id_type=MESH,
        ).start()
        return c

    lax.fori_loop(1, SUBS, send_ids, 0)

    def project(b):
        rows = pl.ds(pl.multiple_of(b * BLOCK, BLOCK), BLOCK)
        fine = jnp.maximum(sums[...], 0.0).astype(BF16).astype(F32)
        fine_rows[rows, :] = fine
        parents = jnp.broadcast_to(parent[pl.ds(b, 1), :], (BLOCK, LANES)).T
        spread = jnp.concatenate(
            [jnp.where(parents == p, fine, 0.0).astype(BF16) for p in range(8)], 1
        )
        down_rows[rows, :] = jnp.dot(spread, w_down[...], preferred_element_type=F32)

    def convolve(b, c):
        def gather(t, c):
            for q in range(GROUP // 8):
                for r in range(8):
                    at = base[b * BLOCK + t * GROUP + q * 8 + r]
                    for k in range(KVOL):
                        row = maps.at[pl.ds(at + ((k // 8) * 32768 + (k % 8) * LANES), 1)][0]
                        held[t * (GROUP // 8) + q, k, r : r + 1, :] = table[pl.ds(row, 1), :]
            return c

        lax.fori_loop(0, BLOCK // GROUP, gather, 0)
        project(jnp.maximum(b - 1, 0))
        wide = jnp.concatenate(
            [held[:, k].reshape(BLOCK, WIDTH).astype(BF16) for k in range(KVOL)], 1
        )
        own = held[:, KVOL // 2].reshape(BLOCK, WIDTH)
        sums[...] = own + jnp.dot(wide, w_sub[...], preferred_element_type=F32)
        return c

    def send_part(j):
        low, high = PARTS[j]
        count = high - low
        source, landing, first = (near_out, near_in, low) if high <= LANES else (far_out, far_in, 0)

        def one(d, c):
            peer = lax.rem(me + d, SUBS)
            if high <= LANES:
                pull(count, lambda r: near[peer * LANES + first + r], down_rows, stage)
            else:
                shift = 32 * lax.rem(me, 4)
                pull(count, lambda r: far[peer * LANES + shift + r], down_rows, stage)
            source[peer, first : first + count, :] = stage[0:count, :].astype(BF16)
            pltpu.make_async_remote_copy(
                src_ref=source.at[peer, pl.ds(first, count)],
                dst_ref=landing.at[me, pl.ds(first, count)],
                send_sem=part_send.at[j], recv_sem=part_recv.at[j],
                device_id=(region, peer), device_id_type=MESH,
            ).start()
            return c

        lax.fori_loop(1, SUBS, one, 0)

    start = 0
    for j, stop in enumerate(AFTER):
        lax.fori_loop(start, stop, convolve, 0)
        send_part(j)
        start = stop
    project(VOX // BLOCK - 1)
    send_part(5)

    def put_back(t, c):
        pull(64, lambda r: place[t * 64 + r], fine_rows, stage)
        fine_out[pl.ds(pl.multiple_of(t * 64, 64), 64), :] = stage[...].astype(BF16)
        return c

    lax.fori_loop(0, VOX // 64, put_back, 0)

    def accumulate(lane_ids, rows):
        hits = jnp.concatenate(
            [
                jnp.where(iota((CV, LANES), 0) + 1 == row, 1.0, 0.0).astype(BF16)
                for row in lane_ids
            ],
            1,
        )
        total[...] += jnp.dot(hits, rows, preferred_element_type=F32)

    def add_local(q, c):
        block = down_rows[pl.ds(pl.multiple_of(q * 1024, 1024), 1024), :].astype(BF16)
        eight = local[pl.ds(pl.multiple_of(q * 8, 8), 8), :]
        accumulate([eight[i : i + 1] for i in range(8)], block)
        return c

    lax.fori_loop(0, 4, add_local, 0)
    settle(ids_in.at[others], ids_recv)
    ids_in[me] = jnp.zeros((2, LANES), I32)
    for j, (low, high) in enumerate(PARTS[:-1]):
        settle(near_in.at[others, pl.ds(low, high - low)], part_recv.at[j])

    def add_near(q, c):
        block = near_in[pl.ds(q * 8, 8)].reshape(1024, WIDTH)
        accumulate([ids_in[q * 8 + i, 0:1, :] for i in range(8)], block)
        return c

    lax.fori_loop(0, 4, add_near, 0)
    settle(far_in.at[others], part_recv.at[5])
    lane_ids = [
        ids_in[4 * i, 1:2, :] + ids_in[4 * i + 1, 1:2, :]
        + ids_in[4 * i + 2, 1:2, :] + ids_in[4 * i + 3, 1:2, :]
        for i in range(8)
    ]
    accumulate(lane_ids, far_in[...].reshape(1024, WIDTH))
    coarse_out[...] = total[...].astype(BF16)
    settle(list_out.at[others], list_send)
    settle(ids.at[others], ids_send)
    for j, (low, high) in enumerate(PARTS[:-1]):
        settle(near_out.at[others, pl.ds(low, high - low)], part_send.at[j])
    settle(far_out.at[others], part_send.at[5])


def per_device(
    features, face_rows, sub_send, neighbors, w_sub, parent_position, coarse_target, w_down
):
    me = lax.axis_index("sub").astype(I32)
    base, local, parent, place, near, far, ids = plan(me, coarse_target, parent_position)
    moved = jnp.transpose(neighbors)
    moved = jnp.where(moved > PAD, moved + (RECV - PAD - 1), moved)
    maps = jnp.pad(moved, ((0, 32 - KVOL), (0, 0)))
    maps = maps.reshape(4, 8, VOX // LANES, LANES).transpose(0, 2, 1, 3).reshape(-1)
    vmem, anywhere = pl.BlockSpec(memory_space=pltpu.VMEM), pl.BlockSpec(memory_space=pl.ANY)
    dma = pltpu.SemaphoreType.DMA
    line = pltpu.SMEM((VOX,), I32)
    return pl.pallas_call(
        main_kernel,
        out_shape=(
            jax.ShapeDtypeStruct((VOX, WIDTH), BF16),
            jax.ShapeDtypeStruct((CV, WIDTH), BF16),
        ),
        in_specs=[anywhere] * 8 + [vmem] * 5,
        out_specs=(vmem, vmem),
        scratch_shapes=[
            pltpu.VMEM((VOX, WIDTH), BF16),
            pltpu.SMEM((2, HALO), I32),
            pltpu.SMEM((SUBS, CAP), I32),
            pltpu.SMEM((32 * VOX,), I32),
            line, line, line, line,
            pltpu.VMEM((ROWS, WIDTH), F32),
            pltpu.VMEM((64, WIDTH), F32),
            pltpu.VMEM((BLOCK // 8, KVOL, 8, WIDTH), F32),
            pltpu.VMEM((BLOCK, WIDTH), F32),
            pltpu.VMEM((VOX, WIDTH), F32),
            pltpu.VMEM((VOX + 8, WIDTH), F32),
            pltpu.VMEM((2 * HALO, WIDTH), BF16),
            pltpu.VMEM((2 * HALO, WIDTH), BF16),
            pltpu.VMEM((SUBS, CAP, WIDTH), BF16),
            pltpu.VMEM((SUBS, CAP, WIDTH), BF16),
            pltpu.VMEM((SUBS, 2, LANES), I32),
            pltpu.VMEM((SUBS, LANES, WIDTH), BF16),
            pltpu.VMEM((SUBS, LANES, WIDTH), BF16),
            pltpu.VMEM((SUBS, 32, WIDTH), BF16),
            pltpu.VMEM((SUBS, 32, WIDTH), BF16),
            pltpu.VMEM((CV, WIDTH), F32),
            dma((8,)), dma((2,)), dma((2,)), dma, dma, dma, dma, dma((6,)), dma((6,)),
        ],
        compiler_params=pltpu.CompilerParams(
            collective_id=0, has_side_effects=True, vmem_limit_bytes=48 << 20
        ),
        name="sparse_convolution",
    )(
        features, face_rows, sub_send, maps,
        base.reshape(-1), place.reshape(-1), near.reshape(-1), far.reshape(-1),
        local, parent, ids, w_sub, w_down,
    )


def solution(mesh):
    split, whole = P(("region", "sub"), None), P()
    line = P(("region", "sub"))
    return jax.shard_map(
        per_device,
        mesh=mesh,
        in_specs=(split, split, split, split, whole, line, line, whole),
        out_specs=(split, split),
        check_vma=False,
    )
```

time: 741 us -> 135 us (0.18)
  local copies, waits for them, and re-layouts: 366 us -> 4.81 us
  waiting for transfers between devices: 231 us -> 0 us
  Pallas kernels: 0 us -> 127 us
  matrix products: 59.3 us -> 0 us
  other arithmetic: 50.9 us -> 1.23 us
  starting transfers between devices: 17.3 us -> 0 us
  between operations: 14.3 us -> 0.71 us
    gather x14 -> x0, local copies, waits for them, and re-layouts: 289 us -> none  [the longest x8 228 us: one_block(): gathered = full_table[map_block].reshape(block_rows, -1)]
    reduce_scatter x1 -> x0, waiting for transfers between devices: 230 us -> none  [per_device(): summed = lax.psum_scatter(spread, 'sub', scatter_dimension=0, tiled=True)]
    pallas_call x0 -> x2, Pallas kernels: none -> 127 us  [the longest x1 126 us: per_device(): pl.pallas_call(main_kernel, out_shape=(jax.ShapeDtypeStruct((VOX, WIDTH),...]
    reshape x10 -> x0, local copies, waits for them, and re-layouts: 61.2 us -> none  [the longest x8 60.4 us: one_block(): gathered = full_table[map_block].reshape(block_rows, -1)]
    dot_general x19 -> x0, matrix products: 59.3 us -> none  [the longest x8 31.8 us: one_block(): summed = jnp.dot(gathered, w_sub, preferred_element_type=jnp.float32)]
    select_n x21 -> x1, other arithmetic: 30 us -> 1.23 us  [per_device(): moved = jnp.where(moved > PAD, moved + (RECV - PAD - 1), moved)]
    reduce_max x8 -> x0, other arithmetic: 12.1 us -> none  [step(): jnp.max(jnp.where(hit, row_ids[None, :], -1), 1)]
    all_to_all x1 -> x0, starting transfers between devices: 11.5 us -> none  [per_device(): lax.all_to_all(outgoing, 'sub', split_axis=0, concat_axis=0, tiled=True)]
  transfers between devices with their start and end apart: 4 -> 0, of which waited for: 1 -> 0; matrix products, arithmetic and copies ran while one was open for 9% -> 0% of each run, Pallas kernels for 0% -> 0%
where the time goes in v1:
time: 135 us; the launch traced here: 134 us
  Pallas kernels  127 us (94%)
  local copies, waits for them, and re-layouts  4.81 us (4%)
    pallas_call x1, Pallas kernels, per_device(): pl.pallas_call(main_kernel, out_shape=(jax.ShapeDtypeStruct((VOX, WIDTH),...  126 us
    unnamed x16, local copies, waits for them, and re-layouts  4.77 us

profile of v1, /device:TPU:2, one launch (start us, length us, event | category | flops | bytes accessed | tf_op | source)
XLA Modules:
  0.0 134.1 jit_solution(2334453644704643199)
XLA Ops:
  0.6 0.0 copy-start.4
  0.6 0.7 copy-done.4
  1.4 0.0 copy-start.5
  1.4 0.7 copy-done.5
  2.1 1.9 %plan.1 = (s32[32,128]{1,0:T(8,128)S(1)}, s32[32,128]{1,0:T(8,128)S(1)}, f32[32,128]{1,0:T(8,128)S(1)}, s32[1,4096]{1,0:T(1,128)S(1)}, s32[32,128]{1,0:T(8,128)S...) custom-call(s32[1]{0:T(128)} %bitcast.4.me_ref, s32[1,4096]{1,0:T(1,128)S(1)} %bitcast.19, s32[1,4096]{1,0:T(1,128)S(1)} %bitcast.20), custom_call_target="tpu_custom_call" | custom-call | tf_op jit(solution)/shard_map/plan/pallas_call | solution.py:97
  4.0 0.0 copy-start
  4.0 0.0 copy-start.1
  4.0 1.2 compare_select_fusion
  5.2 0.0 copy-start.3
  5.2 0.0 copy-start.6
  5.3 0.1 copy-done
  5.3 0.3 copy-done.1
  5.6 0.4 copy-done.3
  6.0 0.0 copy-done.6
  6.0 0.0 copy-start.2
  6.0 0.9 copy-done.2
  7.0 125.5 %sparse_convolution.1 = (bf16[4096,128]{1,0:T(8,128)(2,1)S(1)}, bf16[512,128]{1,0:T(8,128)(2,1)S(1)}) custom-call(bf16[4096,128]{1,0:T(8,128)(2,1)S(1)} %copy-done, s32[2,256]{1,0:T(2,128)S(1)} %copy-done.6, s32[32,64]{1,0:T(8,128)S(1)} %copy-done.3, s32[131072]{0:T(1024)S(1)} %bitcast.14, s32[4096]{0:T(1024)S(1)} %bitcast.15, s32[4096]{0:T(1024)S(1)} %bitcast.16, ...), custom_call_target="tpu_custom_call" | custom-call | tf_op jit(solution)/shard_map/sparse_convolution/pallas_call | solution.py:356
  132.5 1.0 copy.12
  133.5 0.7 copy.13
  (1 shorter events, 0.0 us)
Async XLA Ops:
  0.6 0.7 copy-start.4
  1.4 0.7 copy-start.5
  4.0 1.4 %copy-start = (bf16[4096,128]{1,0:T(8,128)(2,1)S(1)}, bf16[4096,128]{1,0:T(8,128)(2,1)}, u32[]{:S(2)}) copy-start(bf16[4096,128]{1,0:T(8,128)(2,1)} %feat_hbm.1) | copy-start | bytes 3145732
  4.0 1.6 %copy-start.1 = (bf16[3456,128]{1,0:T(8,128)(2,1)S(1)}, bf16[3456,128]{1,0:T(8,128)(2,1)}, u32[]{:S(2)}) copy-start(bf16[3456,128]{1,0:T(8,128)(2,1)} %w_sub.1) | copy-start | bytes 2654212
  5.2 0.8 copy-start.3
  5.2 0.8 copy-start.6
  6.0 1.0 copy-start.2
